TPU v7x, 32 devices: a whole 2x2x4 slice. The times are simulated.
32 devices in a mesh: dp: 8 (over z, y), fsdp: 4 (over x, core).
Axes of the slice: x: 2, y: 2, z: 4, core: 2. Of those that a mesh axis runs over, the one named last changes fastest.
Arguments:
- buf_states: float32 [2048, 11], P(('dp', 'fsdp')), may hold values from -6 to 6
- buf_actions: float32 [2048, 3], P(('dp', 'fsdp')), may hold values from -0.95 to 0.95
- buf_returns: float32 [2048], P(('dp', 'fsdp')), may hold values from -6 to 6
- window_starts: int32 [512], P(('dp', 'fsdp')), may hold values from 0 to 44, as said below
- window_repeats: int32 [512], P(('dp', 'fsdp')), may hold values from 1 to 5
- valid_steps: int32 [512, 20], P(('dp', 'fsdp')), may hold values from 0 to 1, as said below
- matrix_groups: int32 [3, 4], replicated, may hold values from 0 to 2
- log_temp: float32 [1], replicated, may hold values from -2 to 0
- small_rows: float32 [85, 512], replicated
- head_bias: float32 [6], replicated, may hold values from -1.5 to 1.5
- qkv_weight: float32 [3, 512, 1536], P(None, ('dp', 'fsdp')), may hold values from -0.25 to 0.25
- out_weight: float32 [3, 512, 512], P(None, ('dp', 'fsdp')), may hold values from -0.5 to 0.5
- up_weight: float32 [3, 512, 2048], P(None, ('dp', 'fsdp')), may hold values from -0.25 to 0.25
- down_weight: float32 [3, 2048, 512], P(None, ('dp', 'fsdp')), may hold values from -0.125 to 0.125
- small_first: float32 [85, 512], replicated, may hold values from -0.005859375 to 0.005859375
- bias_first: float32 [6], replicated, may hold values from -0.005859375 to 0.005859375
- qkv_first: float32 [3, 512, 1536], P(None, ('dp', 'fsdp')), may hold values from -0.001953125 to 0.001953125
- out_first: float32 [3, 512, 512], P(None, ('dp', 'fsdp')), may hold values from -0.001953125 to 0.001953125
- up_first: float32 [3, 512, 2048], P(None, ('dp', 'fsdp')), may hold values from -0.001953125 to 0.001953125
- down_first: float32 [3, 2048, 512], P(None, ('dp', 'fsdp')), may hold values from -0.001953125 to 0.001953125
- small_second: float32 [85, 512], replicated, may hold values from 4.1007996e-07 to 1.6424391e-06
- bias_second: float32 [6], replicated, may hold values from 4.1007996e-07 to 1.6424391e-06
- qkv_second: float32 [3, 512, 1536], P(None, ('dp', 'fsdp')), may hold values from 4.556444e-08 to 1.8225776e-07
- out_second: float32 [3, 512, 512], P(None, ('dp', 'fsdp')), may hold values from 4.556444e-08 to 1.8225776e-07
- up_second: float32 [3, 512, 2048], P(None, ('dp', 'fsdp')), may hold values from 4.556444e-08 to 1.8225776e-07
- down_second: float32 [3, 2048, 512], P(None, ('dp', 'fsdp')), may hold values from 4.556444e-08 to 1.8225776e-07
Outputs:
- totals: float32 [3], replicated
- grad_norm: float32 [1], replicated
- next_temp: float32 [1], replicated
- small_next: float32 [85, 512], replicated
- small_first_next: float32 [85, 512], replicated
- small_second_next: float32 [85, 512], replicated
- bias_next: float32 [6], replicated
- bias_first_next: float32 [6], replicated
- bias_second_next: float32 [6], replicated
- qkv_next: float32 [3, 512, 1536], P(None, ('dp', 'fsdp'))
- out_next: float32 [3, 512, 512], P(None, ('dp', 'fsdp'))
- up_next: float32 [3, 512, 2048], P(None, ('dp', 'fsdp'))
- down_next: float32 [3, 2048, 512], P(None, ('dp', 'fsdp'))
- qkv_copy: bfloat16 [3, 512, 1536], P(None, ('dp', 'fsdp'))
- out_copy: bfloat16 [3, 512, 512], P(None, ('dp', 'fsdp'))
- up_copy: bfloat16 [3, 512, 2048], P(None, ('dp', 'fsdp'))
- down_copy: bfloat16 [3, 2048, 512], P(None, ('dp', 'fsdp'))
- qkv_first_next: float32 [3, 512, 1536], P(None, ('dp', 'fsdp'))
- out_first_next: float32 [3, 512, 512], P(None, ('dp', 'fsdp'))
- up_first_next: float32 [3, 512, 2048], P(None, ('dp', 'fsdp'))
- down_first_next: float32 [3, 2048, 512], P(None, ('dp', 'fsdp'))
- qkv_second_next: float32 [3, 512, 1536], P(None, ('dp', 'fsdp'))
- out_second_next: float32 [3, 512, 512], P(None, ('dp', 'fsdp'))
- up_second_next: float32 [3, 512, 2048], P(None, ('dp', 'fsdp'))
- down_second_next: float32 [3, 2048, 512], P(None, ('dp', 'fsdp'))
Inputs may be any that keep to these rules, and one draw needn't show every extreme that they name: Window w reads rows of the buffer block of the device that holds it: (w // 16) * 64 + window_starts[w] + t. `valid_steps`: in each window the ones follow the zeros and the last timestep is 1.
All inputs are finite; a program needn't handle non-finite values.
Results may differ from a plain program's by a relative error of at most 0.0034.
The roundings to bfloat16 on the way count: a program that leaves them out, or rounds other values in their place, can miss the bound.
Values may be sent and summed in bfloat16 or wider, within the bound.
A program may use at most 256 MiB of HBM per device.

v0:
```python
import math

import jax
import jax.numpy as jnp
from jax import lax
from jax.experimental import pallas as pl
from jax.experimental.pallas import tpu as pltpu
from jax.sharding import PartitionSpec as P

D = 512
H = 8
HD = 64
FF = 2048
S = 11
A = 3
K = 20
STEP = 10

EPS = 1e-05
CLIP = 1.0
LEARN = 0.03
BETA_ONE = 0.5
BETA_TWO = 0.7
DECAY = 0.01
ADAM_EPS = 1e-08
TEMP_RATE = 0.1
MASKED = -1e30
HALF_LOG_TAU = 0.5 * math.log(2.0 * math.pi)
GELU_C = math.sqrt(2.0 / math.pi)
GELU_A = 0.044715
HIGH = lax.Precision.HIGHEST
LOWER = jnp.bfloat16
WIDE = jnp.float32

LAYERS = 3
WINS = 16
BUF_DEV = 64
SLOT = 64
ROWS = WINS * SLOT
CHUNK = 512
CHUNKS = ROWS // CHUNK
STATE_SLOT = 24
STATES = WINS * STATE_SLOT
BLOCKS = 32
PACK = 192
ATTN, FFN = 64, 128
EMB = S + A + 1 + K + 3
FIN = EMB
HEADW = EMB + 2
BASE = EMB + 2 + 2 * A
PER = 9 + FF // D
NROWS = BASE + LAYERS * PER
SMALL = 96
HEAD_AT = 64
EMB_AT = ROWS - 128
VMEM_BYTES = 64 * 1024 * 1024


def dot(a, b, precision=None):
    return lax.dot_general(
        a, b, (((1,), (0,)), ((), ())), precision=precision, preferred_element_type=WIDE
    )


def dot_nt(a, b, precision=None):
    return lax.dot_general(
        a, b, (((1,), (1,)), ((), ())), precision=precision, preferred_element_type=WIDE
    )


def dot_tn(a, b, precision=None):
    return lax.dot_general(
        a, b, (((0,), (0,)), ((), ())), precision=precision, preferred_element_type=WIDE
    )


def iota(shape, dim):
    return lax.broadcasted_iota(jnp.int32, shape, dim)


def col_sum(v):
    return jnp.sum(v, 0, keepdims=True)


def row_mean(v):
    return jnp.mean(v, -1, keepdims=True)


def norm_parts(x):
    center = x - row_mean(x)
    scale = lax.rsqrt(row_mean(center * center) + EPS)
    return center * scale, scale


def norm_back(xhat, scale, gain, grad):
    scaled = grad * gain
    return scale * (scaled - row_mean(scaled) - xhat * row_mean(scaled * xhat))


def token_rows(at, count):
    row = at + iota((count, 128), 0)
    place = row & (SLOT - 1)
    step = (place * 21846) >> 16
    return row >> 6, step, place - 3 * step, place < 3 * K


def chunk_rows(c):
    return pl.ds(pl.multiple_of(c * CHUNK, CHUNK), CHUNK)


def owner_place(i):
    z, y, x, c = i // 8, (i // 4) % 2, (i // 2) % 2, i % 2
    return 2 * c + x, 4 * y + z


class Kit:
    def __init__(self, **refs):
        self.__dict__.update(refs)

    def row(self, l, k):
        return self.lrows[l, k : k + 1, :]

    def blocks(self, ref, l, first, count, owners):
        places = [owner_place(i) for i in owners]
        return jnp.concatenate([ref[l, a, b, first : first + count, :] for a, b in places], 0)

    def w_qkv(self, l, j):
        return self.blocks(self.wa, l, 16 * j, 16, range(BLOCKS))

    def w_out(self, l):
        return self.blocks(self.wa, l, 48, 16, range(BLOCKS))

    def w_up(self, l, j):
        return self.blocks(self.wf, l, 16 * j, 16, range(BLOCKS))

    def w_down(self, l, j):
        return self.blocks(self.wf, l, 64, 64, range(8 * j, 8 * j + 8))


def slot(l):
    return l % 2


def setup_stage(k):
    k.xs[2, EMB_AT:ROWS, :] = jnp.zeros((128, D), WIDE)
    k.xs[2, EMB_AT : EMB_AT + EMB, :] = k.small[0:EMB, :]
    k.headw[...] = jnp.zeros_like(k.headw)
    k.headw[0, 0:A, :] = k.small[HEADW : HEADW + A, :].astype(LOWER)
    k.headw[1, 0:A, :] = k.small[HEADW + A : HEADW + 2 * A, :].astype(LOWER)
    for l in range(LAYERS):
        k.lrows[l, 0:PER, :] = k.small[BASE + l * PER : BASE + (l + 1) * PER, :]
    k.sgl[...] = jnp.zeros_like(k.sgl)
    k.sgh[...] = jnp.zeros_like(k.sgh)
    k.sgw[...] = jnp.zeros_like(k.sgw)

    lane, sub = iota((WINS, 128), 1), iota((WINS, 128), 0)
    k.meta[...] = jnp.zeros_like(k.meta)
    k.meta[0:WINS, 0:K] = k.valid[...].astype(WIDE)
    meta = k.meta[0:WINS, :]
    for w in range(WINS):
        for n, ref in enumerate((k.starts, k.repeats)):
            meta = jnp.where((sub == w) & (lane == K + n), ref[w].astype(WIDE), meta)
    k.meta[0:WINS, :] = meta
    meta = k.meta[...].astype(LOWER)
    k.buf[...] = jnp.zeros_like(k.buf)
    k.buf[0, 0:S, 0:BUF_DEV] = k.states[...]
    k.buf[0, S + A : S + A + 1, 0:BUF_DEV] = k.returns[...]
    k.buf[1, 0:A, 0:BUF_DEV] = k.actions[...]

    def chunk(c, carry):
        rows = chunk_rows(c)
        win, step, kind, real = token_rows(c * CHUNK, CHUNK)
        lane = iota((CHUNK, 128), 1)
        tok = dot((lane == win).astype(WIDE).astype(LOWER), meta)
        start, repeat = tok[:, K : K + 1], tok[:, K + 1 : K + 2]
        valid = jnp.sum(jnp.where(lane == step, tok, 0.0), -1, keepdims=True)
        key = iota((CHUNK, 128), 0) & (SLOT - 1)
        query = lane & (SLOT - 1)
        allowed = (key <= query) & (((valid > 0.5) & real) | (key == query))
        k.bias[rows, :] = jnp.where(allowed, 0.0, MASKED)
        place = start.astype(jnp.int32) + step
        source = ((lane == place) & real).astype(WIDE)
        raw = dot_nt(source, k.buf[0], HIGH)
        acts = dot_nt(source, k.buf[1], HIGH)
        mine = (
            ((lane < S) & (kind == 1))
            | ((lane >= S) & (lane < S + A) & (kind == 2))
            | ((lane == S + A) & (kind == 0))
        )
        raw = raw + pltpu.roll(acts, S, 1)
        marks = ((lane == S + A + 1 + step) | (lane == S + A + 1 + K + kind)) & real
        feats = jnp.where(mine, raw, 0.0) + marks.astype(WIDE)
        weight = jnp.where((kind == 1) & real, repeat * valid, 0.0)
        acts = pltpu.roll(acts, HEAD_AT, 1)
        ours = (lane >= HEAD_AT) & (lane < HEAD_AT + A)
        feats = jnp.where(ours, acts, jnp.where(lane == HEAD_AT + A, weight, feats))
        k.feats[rows, :] = feats
        k.xs[0, rows, :] = dot(feats, k.xs[2, EMB_AT:ROWS, :], HIGH)
        return carry

    lax.fori_loop(0, CHUNKS, chunk, 0)


def stack_pair(v, first):
    zero = jnp.zeros_like(v)
    return jnp.concatenate([jnp.where(first, v, zero), jnp.where(first, zero, v)], 0)


def join_pair(v, first):
    return jnp.where(first, v[:SLOT], v[SLOT:])


def window_rows(w):
    return pl.ds(pl.multiple_of(w * SLOT, SLOT), SLOT)


def each_chunk(body, between=None):
    def step(c, carry):
        body(c, chunk_rows(c))
        if between is not None:

            @pl.when(c < CHUNKS - 1)
            def _():
                between()

        return carry

    lax.fori_loop(0, CHUNKS, step, 0)


def each_pair(body, between=None):
    def pair(n, carry):
        chains = [
            (2 * n + w, window_rows(2 * n + w), slice(p * 128, (p + 1) * 128))
            for w in range(2)
            for p in range(H // 2)
        ]
        body(pl.ds(pl.multiple_of(n * 128, 128), 128), chains)
        if between is not None:

            @pl.when(n == WINS // 4 - 1)
            def _():
                between()

        return carry

    lax.fori_loop(0, WINS // 2, pair, 0)


def forward_qkv(k, l, between):
    def chunk(c, rows):
        xhat, _ = norm_parts(k.xs[slot(l), rows, :])
        normed = (xhat * k.row(l, 0) + k.row(l, 1)).astype(LOWER)
        k.normed_t[:, rows] = normed.T
        for j in range(3):
            part = dot(normed, k.w_qkv(l, j)) + k.row(l, 4 + j)
            k.qkv[rows, j * D : (j + 1) * D] = part.astype(LOWER)

    each_chunk(chunk, between)


def qkv_part(k, n, rows, at):
    return k.qkv[rows, n * D + at.start : n * D + at.stop]


def forward_windows(k, l, between):
    first = iota((SLOT, 128), 1) < HD
    scale = jnp.asarray(HD**-0.5, LOWER)

    def pair(both, chains):
        query = [stack_pair(qkv_part(k, 0, rows, at) * scale, first) for _, rows, at in chains]
        scores = [
            dot_nt(qkv_part(k, 1, rows, at), q) + k.bias[rows, :]
            for q, (_, rows, at) in zip(query, chains)
        ]
        peaks = [jnp.max(s, 0, keepdims=True) for s in scores]
        expos = [jnp.exp(s - peak) for s, peak in zip(scores, peaks)]
        totals = [jnp.sum(e, 0, keepdims=True) for e in expos]
        probs = [(e * (1.0 / total)).astype(LOWER) for e, total in zip(expos, totals)]
        outs = [dot_tn(p, qkv_part(k, 2, rows, at)) for p, (_, rows, at) in zip(probs, chains)]
        for peak, total, out, (w, rows, at) in zip(peaks, totals, outs, chains):
            p = at.start // 128
            k.logs[l, w, p : p + 1, :] = peak + jnp.log(total)
            k.left[rows, at] = join_pair(out, first).astype(LOWER)
        k.mixed_t[:, both] = k.left[both, :].T

    each_pair(pair, between)


TILES = [slice(n * 128, (n + 1) * 128) for n in range(D // 128)]


def load_mid(k, rows):
    return jnp.concatenate([k.mid[n, rows, :] for n in range(len(TILES))], 1)


def store_mid(k, rows, value):
    for n, tile in enumerate(TILES):
        k.mid[n, rows, :] = value[:, tile]


def take_states(src, dst, cols):
    dst[0:STATES, cols] = jnp.zeros((STATES, 128), WIDE)
    for w in range(WINS):
        rows = slice(w * STATE_SLOT, w * STATE_SLOT + K)
        dst[rows, cols] = src[pl.ds(w * SLOT + 1, K, stride=3), :]


def put_states(k, value):
    for n, tile in enumerate(TILES):
        dst = k.mid.at[n]
        dst[...] = jnp.zeros((ROWS, 128), WIDE)
        for w in range(WINS):
            rows = slice(w * STATE_SLOT, w * STATE_SLOT + K)
            dst[pl.ds(w * SLOT + 1, K, stride=3), :] = value[rows, tile]


def forward_up(k, l, between):
    each_chunk(lambda c, rows: up_rows(k, l, rows, k.xs[slot(l), rows, :], k.left[rows, :]), between)


def up_rows(k, l, rows, x, mixed):
    mid = x + dot(mixed, k.w_out(l)) + k.row(l, 7)
    store_mid(k, rows, mid)
    xhat, _ = norm_parts(mid)
    second = (xhat * k.row(l, 2) + k.row(l, 3)).astype(LOWER)
    k.second_t[:, rows] = second.T
    ahead = dot(second, k.w_up(l, 0))
    for j in range(4):
        cols = slice(j * D, (j + 1) * D)
        h = ahead + k.row(l, 8 + j)
        if j < 3:
            ahead = dot(second, k.w_up(l, j + 1))
        square = h * h
        over = 1.0 + jnp.tanh(h * (GELU_C + GELU_C * GELU_A * square))
        half = 0.5 * h
        acted = (half * over).astype(LOWER)
        slope = over * (0.5 + half * (2.0 - over) * (GELU_C + 3.0 * GELU_A * GELU_C * square))
        k.work[rows, cols] = acted
        k.slope[rows, cols] = slope.astype(LOWER)
        k.act_t[cols, rows] = acted.T


def forward_down(k, l, dest):
    each_chunk(lambda c, rows: down_rows(k, l, rows, dest))


def down_rows(k, l, rows, dest):
    w_down = jnp.concatenate([k.w_down(l, j) for j in range(4)], 0)
    k.xs[dest, rows, :] = load_mid(k, rows) + k.row(l, 12) + dot(k.work[rows, :], w_down)


def forward_up_states(k, l, spare):
    every, rows = slice(0, ROWS), slice(0, STATES)
    store_mid(k, every, k.left[...].astype(WIDE))
    for n, tile in enumerate(TILES):
        take_states(k.mid.at[n], k.xs.at[spare], tile)
    mixed = k.xs[spare, rows, :].astype(LOWER)
    k.mixed_t[:, rows] = mixed.T
    store_mid(k, every, k.xs[slot(l)])
    for n, tile in enumerate(TILES):
        take_states(k.mid.at[n], k.xs.at[spare], tile)
    up_rows(k, l, rows, k.xs[spare, rows, :], mixed)


def head_stage(k, at):
    gain, bias = k.small[FIN : FIN + 1, :], k.small[FIN + 1 : FIN + 2, :]
    lane = iota((STATES, 128), 1)
    keep = lane < A

    def bias_row(first):
        row = jnp.zeros((1, 128), WIDE)
        at = iota((1, 128), 1)
        for a in range(A):
            row = jnp.where(at == a, k.head_bias[first + a], row)
        return row

    bias_mean, bias_spread = bias_row(0), bias_row(A)
    temp = jnp.exp(jnp.full((1, 128), k.log_temp[0], WIDE))

    rows = slice(0, STATES)
    xhat, scale = norm_parts(k.xs[at, rows, :])
    feats = (xhat * gain + bias).astype(LOWER)
    mean = dot_nt(feats, k.headw[0]) + bias_mean
    spread = jnp.tanh(dot_nt(feats, k.headw[1]) + bias_spread)
    take_states(k.feats, k.heads, slice(0, 128))
    acts = pltpu.roll(k.heads[...], 128 - HEAD_AT, 1)
    weight = acts[:, A : A + 1]
    acts = jnp.where(keep, acts, 0.0)
    target = 0.5 * (jnp.log(1.0 + acts) - jnp.log(1.0 - acts))
    shrink = jnp.exp(-spread)
    zed = (target - mean) * shrink
    terms = 0.5 * zed * zed + spread + HALF_LOG_TAU + jnp.log(1.0 - acts * acts)
    nll = jnp.sum(jnp.where(keep, terms, 0.0), -1, keepdims=True)
    entropy = jnp.sum(jnp.where(keep, spread, 0.0), -1, keepdims=True) + A * (0.5 + HALF_LOG_TAU)
    loss = weight * (nll - temp * entropy)
    sums = jnp.where(lane == 0, loss, jnp.where(lane == 1, weight * entropy, jnp.where(lane == 2, weight, 0.0)))
    d_mean = jnp.where(keep, weight * (-zed * shrink), 0.0).astype(LOWER)
    d_spread = weight * (1.0 - zed * zed - temp) * (1.0 - spread * spread)
    d_spread = jnp.where(keep, d_spread, 0.0).astype(LOWER)
    k.sgh[2:3, 0:128] += col_sum(sums)
    k.sgh[3:4, 0:128] += col_sum(d_mean.astype(WIDE))
    k.sgh[4:5, 0:128] += col_sum(d_spread.astype(WIDE))
    k.sgw[0] += dot_tn(d_mean, feats)[0:8]
    k.sgw[1] += dot_tn(d_spread, feats)[0:8]
    d_feats = dot(d_mean, k.headw[0]) + dot(d_spread, k.headw[1])
    k.sgh[0:1, :] += col_sum(d_feats * xhat)
    k.sgh[1:2, :] += col_sum(d_feats)
    k.xs[at, rows, :] = norm_back(xhat, scale, gain, d_feats)


def store_blocks(ref, l, owners, first, count, value):
    value = value.astype(LOWER)
    for n, i in enumerate(owners):
        a, b = owner_place(i)
        ref[l, a, b, first : first + count, :] = value[n * count : (n + 1) * count]


def backward_ffn(k, l, grad, between=None):
    each_chunk(lambda c, rows: ffn_back_rows(k, l, rows, grad), between)


def ffn_back_rows(k, l, rows, grad):
    d_down = k.xs[grad, rows, :].astype(LOWER)
    k.dout[rows, :] = d_down
    k.sgl[l, 12:13, :] += col_sum(d_down.astype(WIDE))
    d_second = jnp.zeros(d_down.shape, WIDE)
    ahead = dot_nt(d_down, k.w_down(l, 0))
    for j in range(4):
        cols = slice(j * D, (j + 1) * D)
        d_acted = ahead
        if j < 3:
            ahead = dot_nt(d_down, k.w_down(l, j + 1))
        d_hidden = (d_acted * k.slope[rows, cols].astype(WIDE)).astype(LOWER)
        k.work[rows, cols] = d_hidden
        k.sgl[l, 8 + j : 9 + j, :] += col_sum(d_hidden.astype(WIDE))
        d_second = d_second + dot_nt(d_hidden, k.w_up(l, j))
    xhat, scale = norm_parts(load_mid(k, rows))
    k.sgl[l, 2:3, :] += col_sum(d_second * xhat)
    k.sgl[l, 3:4, :] += col_sum(d_second)
    k.xs[grad, rows, :] += norm_back(xhat, scale, k.row(l, 2), d_second)


def backward_down_grads(k, l, rows=slice(0, ROWS)):
    for j in range(4):
        part = dot(k.act_t[j * D : (j + 1) * D, rows], k.dout[rows, :])
        store_blocks(k.wf, l, range(8 * j, 8 * j + 8), 64, 64, part)


def backward_up_grads(k, l, rows=slice(0, ROWS)):
    for j in range(4):
        part = dot(k.second_t[:, rows], k.work[rows, j * D : (j + 1) * D])
        store_blocks(k.wf, l, range(BLOCKS), 16 * j, 16, part)


def backward_out(k, l, grad):
    def before(c, rows):
        d_branch = k.xs[grad, rows, :].astype(LOWER)
        k.left[rows, :] = d_branch
        k.sgl[l, 7:8, :] += col_sum(d_branch.astype(WIDE))
        k.dout[rows, :] = dot_nt(d_branch, k.w_out(l)).astype(LOWER)

    each_chunk(before)
    store_blocks(k.wa, l + 1, range(BLOCKS), 48, 16, dot(k.mixed_t[...], k.left[...]))


def backward_out_states(k, l, grad):
    rows = slice(0, STATES)
    d_mid = k.xs[grad, rows, :]
    d_branch = d_mid.astype(LOWER)
    k.sgl[l, 7:8, :] += col_sum(d_branch.astype(WIDE))
    d_mixed = dot_nt(d_branch, k.w_out(l)).astype(LOWER)
    store_blocks(k.wa, l + 1, range(BLOCKS), 48, 16, dot(k.mixed_t[:, rows], d_branch))
    put_states(k, d_mixed.astype(WIDE))
    k.dout[...] = load_mid(k, slice(0, ROWS)).astype(LOWER)
    put_states(k, d_mid)
    k.xs[grad] = load_mid(k, slice(0, ROWS))


def backward_windows(k, l, between):
    first = iota((SLOT, 128), 1) < HD
    scale = HD**-0.5
    low = jnp.asarray(scale, LOWER)

    def pair(both, chains):
        query = [stack_pair(qkv_part(k, 0, rows, at) * low, first) for _, rows, at in chains]
        d_mixed = [stack_pair(k.dout[rows, at], first) for _, rows, at in chains]
        shift = [
            k.bias[rows, :] - k.logs[l, w, at.start // 128 : at.start // 128 + 1, :]
            for w, rows, at in chains
        ]
        scores = [dot_nt(qkv_part(k, 1, rows, at), q) for q, (_, rows, at) in zip(query, chains)]
        d_probs = [dot_nt(qkv_part(k, 2, rows, at), d) for d, (_, rows, at) in zip(d_mixed, chains)]
        probs = [jnp.exp(s + more) for s, more in zip(scores, shift)]
        d_values = [dot(p.astype(LOWER), d) for p, d in zip(probs, d_mixed)]
        inner = [p * d for p, d in zip(probs, d_probs)]
        sums = [jnp.sum(i, 0, keepdims=True) for i in inner]
        d_scores = [(i - p * t).astype(LOWER) for i, p, t in zip(inner, probs, sums)]
        d_keyed = [dot(d, q) for d, q in zip(d_scores, query)]
        d_query = [dot_tn(d, qkv_part(k, 1, rows, at)) for d, (_, rows, at) in zip(d_scores, chains)]
        for n, (_, rows, at) in enumerate(chains):
            values = (join_pair(d_query[n], first) * scale, d_keyed[n], d_values[n])
            for m, value in enumerate(values):
                k.work[rows, m * D + at.start : m * D + at.stop] = value.astype(LOWER)

    each_pair(pair, between)


def backward_attn_grads(k, l):
    for j in range(3):
        part = dot(k.normed_t[...], k.work[:, j * D : (j + 1) * D])
        store_blocks(k.wa, l + 1, range(BLOCKS), 16 * j, 16, part)


def backward_input(k, l, grad):
    def chunk(c, rows):
        d_normed = jnp.zeros((CHUNK, D), WIDE)
        for j in range(3):
            d_part = k.work[rows, j * D : (j + 1) * D]
            k.sgl[l, 4 + j : 5 + j, :] += col_sum(d_part.astype(WIDE))
            d_normed = d_normed + dot_nt(d_part, k.w_qkv(l, j))
        xhat, scale = norm_parts(k.xs[slot(l), rows, :])
        k.sgl[l, 0:1, :] += col_sum(d_normed * xhat)
        k.sgl[l, 1:2, :] += col_sum(d_normed)
        k.xs[grad, rows, :] += norm_back(xhat, scale, k.row(l, 0), d_normed)

    each_chunk(chunk)


def small_stage(k, out, grad):
    out[...] = jnp.zeros_like(out)
    out[0:EMB, :] = dot_tn(k.feats[...], k.xs[grad], HIGH)[0:EMB]
    out[FIN : FIN + 2, :] = k.sgh[0:2, :]
    out[HEADW : HEADW + A, :] = k.sgw[0, 0:A, :]
    out[HEADW + A : HEADW + 2 * A, :] = k.sgw[1, 0:A, :]
    for l in range(LAYERS):
        out[BASE + l * PER : BASE + (l + 1) * PER, :] = k.sgl[l, 0:PER, :]
    out[NROWS : NROWS + 3, :] = k.sgh[2:5, :]


WORK_SHAPES = dict(
    wa=((LAYERS + 1, 4, 8, ATTN, D), LOWER),
    wf=((LAYERS, 4, 8, FFN, D), LOWER),
    xs=((3, ROWS, D), WIDE),
    qkv=((ROWS, 3 * D), LOWER),
    normed_t=((D, ROWS), LOWER),
    mixed_t=((D, ROWS), LOWER),
    slope=((ROWS, FF), LOWER),
    act_t=((FF, ROWS), LOWER),
    second_t=((D, ROWS), LOWER),
    mid=((D // 128, ROWS, 128), WIDE),
    logs=((LAYERS, WINS, 8, 128), WIDE),
    work=((ROWS, FF), LOWER),
    left=((ROWS, D), LOWER),
    dout=((ROWS, D), LOWER),
    feats=((ROWS, 128), WIDE),
    heads=((STATES, 128), WIDE),
    bias=((ROWS, 128), WIDE),
    headw=((2, 128, D), LOWER),
    lrows=((LAYERS, 16, D), WIDE),
    sgl=((LAYERS, 16, D), WIDE),
    sgh=((8, D), WIDE),
    sgw=((2, 8, D), WIDE),
    meta=((128, 128), WIDE),
    buf=((2, 128, 128), WIDE),
)
KEEP_ATTN = ("qkv", "normed_t", "mixed_t")
KEEP_FFN = ("slope", "act_t", "second_t", "mid")
KEEP = KEEP_ATTN + KEEP_FFN


MESH = pl.DeviceIdType.MESH
NZ, NY, NX, NC = 4, 2, 2, 2
NR = NY * NX * NC
SHARD = PACK
PARTS, DEEP = 3, 64
HALF = DEEP // 2


class Place:
    def __init__(self):
        dp, fsdp = lax.axis_index("dp"), lax.axis_index("fsdp")
        self.z, self.y = dp // NY, dp % NY
        self.x, self.c = fsdp // NC, fsdp % NC
        self.a, self.b = 2 * self.c + self.x, 4 * self.y + self.z
        self.r = 4 * self.y + fsdp
        self.to_z = [(((self.z + d) % NZ) * NY + self.y, fsdp) for d in range(1, NZ)]
        self.odd = self.z % 2
        self.to_pair = ((self.z + 1 - 2 * self.odd) * NY + self.y, fsdp)
        self.plane = []
        for d in range(1, 8):
            y, x, c = [
                1 - v if d & bit else v for v, bit in ((self.y, 4), (self.x, 2), (self.c, 1))
            ]
            self.plane.append((self.z * NY + y, x * NC + c))
        self.to_c, self.to_x, self.to_y = self.plane[0], self.plane[1], self.plane[3]

    def barrier(self):
        sem = pltpu.get_barrier_semaphore()
        for partner in self.plane + self.to_z:
            pl.semaphore_signal(sem, inc=1, device_id=partner, device_id_type=MESH)
        pl.semaphore_wait(sem, len(self.plane) + len(self.to_z))


def remote(src, dst, send, recv, to):
    return pltpu.make_async_remote_copy(
        src_ref=src, dst_ref=dst, send_sem=send, recv_sem=recv, device_id=to, device_id_type=MESH
    )


def part_ref(weights, part):
    return weights[min(part, 1)], (0, 0, DEEP)[part]


class Gather:
    COPIES = 13

    def __init__(self, place, weights, send, recv):
        self.at, self.weights, self.send, self.recv = place, weights, send, recv

    def copy(self, l, part, n):
        at = self.at
        array, row = part_ref(self.weights, part)
        a, b, rows, to = at.a, pl.ds(4 * at.y, 4), pl.ds(row, DEEP), at.to_c
        if n < 3:
            b, to = at.b, at.to_z[n]
        elif n < 5:
            to = (at.to_x, at.to_y)[n - 3]
        if n in (6, 8, 10, 11, 12):
            a = 2 * at.c + 1 - at.x
        if n in (7, 9, 10, 11, 12):
            b = pl.ds(4 * (1 - at.y), 4)
        if n in (6, 7):
            first = row + at.odd * HALF + (n - 6) * (HALF // 2)
            rows = pl.ds(pl.multiple_of(first, HALF // 2), HALF // 2)
            to = (at.to_y, at.to_x)[n - 6]
        if n in (10, 11):
            rows = pl.ds(pl.multiple_of(row + at.odd * HALF, HALF), HALF)
        if n == 11:
            to = at.to_pair
        if n == 12:
            rows = pl.ds(pl.multiple_of(row + (1 - at.odd) * HALF, HALF), HALF)
        ref = array.at[l, a, b, rows, :]
        q = PARTS * l + part
        return remote(ref, ref, self.send.at[q, n], self.recv.at[q, n], to)

    def start(self, l, part, *ns):
        for n in ns:
            self.copy(l, part, n).start()

    def wait(self, l, part, *ns):
        for n in ns:
            self.copy(l, part, n).wait_recv()

    def first(self, l, part):
        self.start(l, part, 0, 1, 2)

    def second(self, l, part):
        self.wait(l, part, 0, 1, 2)
        self.start(l, part, 3, 4, 5)

    def third(self, l, part):
        self.wait(l, part, 3)
        self.start(l, part, 6, 8)
        self.wait(l, part, 4)
        self.start(l, part, 7, 9)

    def fourth(self, l, part):
        self.wait(l, part, 6, 7)
        self.start(l, part, 11, 10)

    def fifth(self, l, part):
        self.wait(l, part, 11)
        self.start(l, part, 12)

    def last(self, l, part):
        self.wait(l, part, 5, 8, 9, 10, 12)

    def sent(self, l, part):
        for n in range(self.COPIES):
            self.copy(l, part, n).wait_send()


class Reduce:
    COPIES = 8

    def __init__(self, place, grads, landing, send, recv, credit):
        self.at, self.grads, self.landing = place, grads, landing
        self.send, self.recv, self.credit = send, recv, credit

    def refs(self, l, part):
        array, row = part_ref(self.grads, part)
        grads = array.at[l + 1 - min(part, 1), :, :, pl.ds(row, DEEP), :]
        return (grads, *self.landing[part])

    def copy(self, l, part, n):
        at, half = self.at, HALF
        g, r0, r1a, r1b, r2, r3 = self.refs(l, part)
        top, low, other = pl.ds(0, half), pl.ds(half, half), pl.ds(4 * (1 - at.y), 4)
        if n == 0:
            src, dst, to = g.at[pl.ds(2 * (1 - at.c), 2)], r0, at.to_c
        elif n == 1:
            src, dst, to = r0.at[1 - at.x, :, top, :], r1a, at.to_x
        elif n == 2:
            src, dst, to = r0.at[:, other, low, :], r1b, at.to_y
        elif n == 3:
            src, dst, to = r1a.at[other], r2.at[:, top, :], at.to_y
        elif n == 4:
            src, dst, to = r1b.at[1 - at.x], r2.at[:, low, :], at.to_x
        else:
            src, dst, to = r2.at[(at.z + n - 4) % NZ], r3.at[n - 5], at.to_z[n - 5]
        q = PARTS * l + part
        return remote(src, dst, self.send.at[q, n], self.recv.at[q, n], to)

    def may_send(self, l, part, *partners):
        @pl.when(l < LAYERS - 1)
        def _():
            for n in partners:
                pl.semaphore_wait(self.credit.at[part, n], 1)

    def allow(self, l, part, *credits):
        at = self.at

        @pl.when(l > 0)
        def _():
            for n, to in credits:
                pl.semaphore_signal(
                    self.credit.at[part, n], inc=1, device_id=to, device_id_type=MESH
                )

    def start(self, l, part):
        self.may_send(l, part, 0)
        self.copy(l, part, 0).start()

    def first(self, l, part):
        at, half = self.at, HALF
        g, r0, _, _, _, _ = self.refs(l, part)
        top, low = pl.ds(0, half), pl.ds(half, half)
        self.copy(l, part, 0).wait_recv()

        x = 1 - at.x
        total = g[2 * at.c + x, :, top].astype(WIDE) + r0[x, :, top].astype(WIDE)
        r0[x, :, top] = total.astype(LOWER)
        self.may_send(l, part, 1, 2)
        self.copy(l, part, 1).start()
        other = pl.ds(4 * (1 - at.y), 4)
        for x in range(NX):
            total = g[2 * at.c + x, other, low].astype(WIDE) + r0[x, other, low].astype(WIDE)
            r0[x, other, low] = total.astype(LOWER)
        self.copy(l, part, 2).start()

    def second(self, l, part):
        at, half = self.at, HALF
        g, r0, r1a, r1b, _, _ = self.refs(l, part)
        top, low = pl.ds(0, half), pl.ds(half, half)

        x, other, column = 1 - at.x, pl.ds(4 * (1 - at.y), 4), pl.ds(4 * at.y, 4)
        self.copy(l, part, 1).wait_recv()
        total = g[at.a, other, top].astype(WIDE) + r0[at.x, other, top].astype(WIDE)
        r1a[other] = (total + r1a[other].astype(WIDE)).astype(LOWER)
        self.may_send(l, part, 6, 7)
        self.copy(l, part, 3).start()
        self.copy(l, part, 2).wait_recv()
        total = g[2 * at.c + x, column, low].astype(WIDE) + r0[x, column, low].astype(WIDE)
        r1b[x] = (total + r1b[x].astype(WIDE)).astype(LOWER)
        self.copy(l, part, 4).start()

    def chip_sums(self, l, part, z):
        at, half = self.at, HALF
        g, r0, r1a, r1b, r2, _ = self.refs(l, part)
        top, low, b = pl.ds(0, half), pl.ds(half, half), 4 * at.y + z
        upper = g[at.a, b, top].astype(WIDE) + r0[at.x, b, top].astype(WIDE)
        lower = g[at.a, b, low].astype(WIDE) + r0[at.x, b, low].astype(WIDE)
        return (
            upper + r1a[b].astype(WIDE) + r2[z, top].astype(WIDE),
            lower + r1b[at.x, z].astype(WIDE) + r2[z, low].astype(WIDE),
        )

    def third(self, l, part, out):
        at, half, row = self.at, HALF, DEEP * part
        r2 = self.landing[part][3]
        for n in (3, 4):
            self.copy(l, part, n).wait_recv()
        self.may_send(l, part, 3, 4, 5)
        for n in range(3):
            z = (at.z + n + 1) % NZ
            upper, lower = self.chip_sums(l, part, z)
            r2[z, pl.ds(0, half)] = upper.astype(LOWER)
            r2[z, pl.ds(half, half)] = lower.astype(LOWER)
            self.copy(l, part, 5 + n).start()
        upper, lower = self.chip_sums(l, part, at.z)
        out[l, row : row + half, :] = upper
        out[l, row + half : row + 2 * half, :] = lower
        for n in range(5):
            self.copy(l, part, n).wait_send()
        self.allow(l, part, (0, at.to_c), (1, at.to_x), (2, at.to_y))

    def last(self, l, part, out, squares):
        at, row = self.at, DEEP * part
        r3 = self.landing[part][4]
        rows = slice(row, row + DEEP)
        total = out[l, rows, :]
        for n in range(3):
            self.copy(l, part, 5 + n).wait_recv()
            total = total + r3[n].astype(WIDE)
        out[l, rows, :] = total
        squares[0:1, :] += col_sum(total * total)
        for n in range(5, self.COPIES):
            self.copy(l, part, n).wait_send()
        late = [(6, at.to_x), (7, at.to_y)] + [(5 - n, at.to_z[n]) for n in range(3)]
        self.allow(l, part, *late)


class Total:
    COPIES = 7

    def __init__(self, place, ref, rows, send, recv):
        self.at, self.ref, self.rows = place, ref, rows // 2
        self.send, self.recv = send, recv

    def half(self, n):
        return self.ref.at[pl.ds(pl.multiple_of(n * self.rows, 8), self.rows), :]

    def whole(self):
        return self.ref.at[pl.ds(0, 2 * self.rows), :]

    def copy(self, n):
        at = self.at
        mine, other = self.half(at.c), self.half(1 - at.c)
        src, dst, to = (
            (other, self.half(2), at.to_c),
            (self.half(8), self.half(3), at.to_x),
            (self.half(9), self.half(4), at.to_y),
            (self.half(10), self.half(5), at.to_z[0]),
            (self.half(10), self.half(6), at.to_z[1]),
            (self.half(10), self.half(7), at.to_z[2]),
            (mine, self.half(11), at.to_c),
        )[n]
        return remote(src, dst, self.send.at[n], self.recv.at[n], to)

    def start(self):
        self.copy(0).start()

    def step(self, n):
        self.copy(n).wait_recv()
        own = self.half(self.at.c) if n == 0 else self.half(7 + n)
        self.half(8 + n)[...] = own[...] + self.half(2 + n)[...]
        for m in ((1,), (2,), (3, 4, 5))[n]:
            self.copy(m).start()

    def back(self):
        for m in (3, 4, 5):
            self.copy(m).wait_recv()
        self.copy(0).wait_send()
        total = None
        for z in range(NZ):
            term = self.half(10)[...]
            for n in range(3):
                from_z = (self.at.z + NZ - 1 - n) % NZ
                term = jnp.where(from_z == z, self.half(5 + n)[...], term)
            total = term if total is None else total + term
        self.half(self.at.c)[...] = total
        self.copy(6).start()

    def last(self):
        self.copy(6).wait_recv()
        self.half(1 - self.at.c)[...] = self.half(11)[...]
        for n in range(1, self.COPIES):
            self.copy(n).wait_send()


class Norm:
    COPIES = 10

    def __init__(self, place, plane, column, send, recv):
        self.at, self.plane, self.column = place, plane, column
        self.send, self.recv = send, recv

    def copy(self, n):
        at = self.at
        if n < 7:
            ref, to = self.plane.at[at.r], at.plane[n]
        else:
            ref, to = self.column.at[at.z], at.to_z[n - 7]
        return remote(ref, ref, self.send.at[n], self.recv.at[n], to)

    def start(self, tile):
        self.plane[self.at.r] = tile
        for n in range(7):
            self.copy(n).start()

    def total(self, ref, ns):
        for n in ns:
            self.copy(n).wait_recv()
        total = ref[0]
        for n in range(1, ref.shape[0]):
            total = total + ref[n]
        return total

    def step(self):
        self.column[self.at.z] = self.total(self.plane, range(7))
        for n in range(7, self.COPIES):
            self.copy(n).start()

    def last(self):
        total = self.total(self.column, range(7, self.COPIES))
        for n in range(self.COPIES):
            self.copy(n).wait_send()
        return total


LANDING = (
    (NX, 8, DEEP, D),
    (8, HALF, D),
    (NX, NZ, HALF, D),
    (NZ, DEEP, D),
    (3, DEEP, D),
)


def stage_rows(qkv, out, up, down, l):
    return (
        [(qkv.at[l, :, pl.ds(j * D, D)], 16 * j, 16) for j in range(3)]
        + [(out.at[l], 48, 16)]
        + [(up.at[l, :, pl.ds(j * D, D)], 64 + 16 * j, 16) for j in range(4)]
        + [(down.at[l], 128, 64)]
    )


BEGIN, SETUP, START, QKV_HALF, QKV, WINDOWS_HALF, WINDOWS, UP_HALF, UP, DOWN = range(10)
FIRST, SECOND, THIRD, FOURTH, FIFTH, LAST, SEND = range(7)
GATHER_PLAN = {
    (-1, BEGIN): [(FIRST, 0, 0), (FIRST, 0, 1), (FIRST, 0, 2)],
    (-1, SETUP): [(FIRST, 1, 0), (FIRST, 1, 1), (SECOND, 0, 0)],
    (0, START): [(FIRST, 1, 2), (SECOND, 0, 1), (THIRD, 0, 0), (FOURTH, 0, 0), (SECOND, 0, 2), (THIRD, 0, 1), (FIFTH, 0, 0), (LAST, 0, 0)],
    (0, QKV_HALF): [(SECOND, 1, 0), (FOURTH, 0, 1)],
    (0, QKV): [(FIRST, 2, 0), (THIRD, 0, 2), (FIFTH, 0, 1)],
    (0, WINDOWS_HALF): [(SECOND, 1, 1), (LAST, 0, 1)],
    (0, WINDOWS): [(FIRST, 2, 1), (FOURTH, 0, 2)],
    (0, UP_HALF): [(THIRD, 1, 0), (FIFTH, 0, 2), (SECOND, 1, 2)],
    (0, UP): [(FIRST, 2, 2), (LAST, 0, 2), (FOURTH, 1, 0), (SECOND, 2, 0)],
    (0, DOWN): [(THIRD, 1, 1), (FIFTH, 1, 0)],
    (1, START): [(LAST, 1, 0), (FOURTH, 1, 1)],
    (1, QKV_HALF): [(SECOND, 2, 1)],
    (1, QKV): [(THIRD, 1, 2), (FIFTH, 1, 1)],
    (1, WINDOWS_HALF): [(LAST, 1, 1)],
    (1, WINDOWS): [(SECOND, 2, 2), (FOURTH, 1, 2)],
    (1, UP_HALF): [(THIRD, 2, 0), (FIFTH, 1, 2), (LAST, 1, 2)],
    (1, UP): [(FOURTH, 2, 0)],
    (1, DOWN): [(THIRD, 2, 1), (FIFTH, 2, 0)],
    (2, START): [(LAST, 2, 0), (FOURTH, 2, 1)],
    (2, QKV): [(THIRD, 2, 2), (FIFTH, 2, 1)],
    (2, WINDOWS_HALF): [(LAST, 2, 1)],
    (2, WINDOWS): [(FOURTH, 2, 2)],
    (2, UP): [(FIFTH, 2, 2), (LAST, 2, 2)],
}


def train_kernel(refs, alone):
    k = Kit(**refs)

    def kept(names, l, back):
        copies = []
        for name in names:
            here, there = refs[name], refs["keep_" + name].at[l]
            src, dst = (there, here) if back else (here, there)
            copies.append(pltpu.make_async_copy(src, dst, k.keep_sem.at[KEEP.index(name)]))
        return copies

    def start(copies):
        for copy in copies:
            copy.start()

    def wait(copies):
        for copy in copies:
            copy.wait()

    def kept_x(back):
        here, there = k.xs.at[0], k.keep_x
        src, dst = (there, here) if back else (here, there)
        return [pltpu.make_async_copy(src, dst, k.keep_sem.at[len(KEEP)])]

    arrays = [(l, n) for l in range(LAYERS) for n in (0, 1)]
    parts = [(l, part) for l in range(LAYERS) for part in range(PARTS)]
    weights = (k.wa, k.wf)
    if alone:
        loads = [
            pltpu.make_async_copy((k.all_a, k.all_f)[n].at[l], weights[n].at[l], k.load_sem.at[2 * l + n])
            for l, n in arrays
        ]
        stores = [
            pltpu.make_async_copy(
                weights[n].at[l + 1 - n], (k.grad_a, k.grad_f)[n].at[l], k.load_sem.at[2 * l + n]
            )
            for l, n in arrays
        ]
        start(loads)
    else:
        place = Place()
        gather = Gather(place, weights, k.gather_send, k.gather_recv)
        reduce = Reduce(
            place, weights, k.landing, k.reduce_send, k.reduce_recv, k.credit
        )
        sums = Total(place, k.xs.at[1], SMALL, k.sum_send, k.sum_recv)
        norm = Norm(place, k.norm_plane, k.norm_column, k.norm_send, k.norm_recv)

    def run(plan):
        stages = (
            gather.first,
            gather.second,
            gather.third,
            gather.fourth,
            gather.fifth,
            gather.last,
        )
        for stage, l, part in plan:
            stages[stage](l, part)

    def poll(l, point):
        if alone:
            return
        for layer in range(LAYERS):
            plan = GATHER_PLAN.get((layer, point))
            if plan:

                @pl.when(l == layer)
                def _(plan=plan):
                    run(plan)

    if not alone:
        staged = []
        for l in range(LAYERS):
            for n, (src, row, count) in enumerate(stage_rows(k.qkv_w, k.out_w, k.up_w, k.down_w, l)):
                dst = k.xs.at[2, pl.ds(l * PACK + row, count), :]
                staged.append(pltpu.make_async_copy(src, dst, k.stage_sem.at[l, n]))
        start(staged)
        place.barrier()
        for l in range(LAYERS):
            wait(staged[9 * l : 9 * l + 9])
            row = l * PACK
            for part in range(PARTS):
                array, first = part_ref(weights, part)
                mine = k.xs[2, row + DEEP * part : row + DEEP * (part + 1), :].astype(LOWER)
                array[l, place.a, place.b, first : first + DEEP, :] = mine
                if (FIRST, l, part) in GATHER_PLAN[-1, BEGIN]:
                    gather.first(l, part)
        k.squares_sum[...] = jnp.zeros_like(k.squares_sum)

    setup_stage(k)
    start(kept_x(False))
    if not alone:
        run(GATHER_PLAN[-1, SETUP])

    grad = 2

    def forward(l, carry):
        if alone:
            pltpu.make_async_copy(k.all_a.at[l], k.wa.at[l], k.load_sem.at[2 * l]).wait()

        @pl.when(l > 0)
        def _():
            wait(kept(KEEP_ATTN, l - 1, False))

        poll(l, START)
        forward_qkv(k, l, lambda: poll(l, QKV_HALF))
        poll(l, QKV)
        forward_windows(k, l, lambda: poll(l, WINDOWS_HALF))

        @pl.when(l < LAYERS - 1)
        def _():
            start(kept(KEEP_ATTN, l, False))

        @pl.when(l > 0)
        def _():
            wait(kept(KEEP_FFN, l - 1, False))

        @pl.when(l == 1)
        def _():
            wait(kept_x(False))

        if alone:
            pltpu.make_async_copy(k.all_f.at[l], k.wf.at[l], k.load_sem.at[2 * l + 1]).wait()
        poll(l, WINDOWS)

        @pl.when(l < LAYERS - 1)
        def _():
            forward_up(k, l, lambda: poll(l, UP_HALF))

        @pl.when(l == LAYERS - 1)
        def _():
            forward_up_states(k, l, grad)

        poll(l, UP)

        @pl.when(l < LAYERS - 1)
        def _():
            forward_down(k, l, (l + 1) % 2)

        @pl.when(l == LAYERS - 1)
        def _():
            down_rows(k, l, slice(0, STATES), grad)

        @pl.when(l < LAYERS - 1)
        def _():
            start(kept(KEEP_FFN, l, False))

        poll(l, DOWN)
        return carry

    lax.fori_loop(0, LAYERS, forward, 0)
    if not alone:
        for l, part in parts:
            gather.sent(l, part)
    head_stage(k, grad)

    def run_reduce(stage, l, part):
        if stage == THIRD:
            reduce.third(l, part, k.shard)
        elif stage == LAST:
            reduce.last(l, part, k.shard, k.squares_sum)
        else:
            {SEND: reduce.start, FIRST: reduce.first, SECOND: reduce.second}[stage](l, part)

    def backward(n, carry):
        l = LAYERS - 1 - n

        def behind(name, *stages):
            @pl.when(n > 0)
            def _():
                for stage, part, *more in stages:
                    stage(l + 1, part, *more)

        @pl.when(n > 0)
        def _():
            wait(kept(KEEP_FFN, l, True))

        def now(stage, part, early=None):
            if alone:
                return
            if early is None:
                run_reduce(stage, l, part)
                return

            @pl.when((n == LAYERS - 1) if early else (n < LAYERS - 1))
            def _():
                run_reduce(stage, l, part)

        def then(stage, part):
            if not alone:

                @pl.when(n > 0)
                def _():
                    run_reduce(stage, l + 1, part)

        def in_ffn():
            then(LAST, 2)
            then(THIRD, 1)
            then(FIRST, 0)

        def in_windows():
            now(FIRST, 1, False)
            now(SECOND, 2, True)

        states = slice(0, STATES)

        @pl.when(n > 0)
        def _():
            backward_ffn(k, l, grad, in_ffn)
            backward_down_grads(k, l)

        @pl.when(n == 0)
        def _():
            ffn_back_rows(k, l, states, grad)
            backward_down_grads(k, l, states)

        now(SEND, 2)
        then(LAST, 1)
        then(SECOND, 0)

        @pl.when(n > 0)
        def _():
            backward_up_grads(k, l)

        @pl.when(n == 0)
        def _():
            backward_up_grads(k, l, states)

        @pl.when((n > 0) & (n < LAYERS - 1))
        def _():
            start(kept(KEEP_FFN, l - 1, True))

        now(SEND, 1)
        now(FIRST, 2, True)

        @pl.when(n > 0)
        def _():
            wait(kept(KEEP_ATTN, l, True))

        @pl.when(n > 0)
        def _():
            backward_out(k, l, grad)

        @pl.when(n == 0)
        def _():
            backward_out_states(k, l, grad)
            start(kept(KEEP_FFN, l - 1, True))

        now(FIRST, 2, False)
        now(FIRST, 1, True)
        then(THIRD, 0)
        backward_windows(k, l, in_windows)
        now(SECOND, 2, False)
        now(THIRD, 2, True)
        then(LAST, 0)
        backward_attn_grads(k, l)

        @pl.when(n < LAYERS - 1)
        def _():
            start(kept(KEEP_ATTN, l - 1, True))

        now(SEND, 0)
        now(THIRD, 2, False)
        now(SECOND, 1, True)

        @pl.when(n == LAYERS - 1)
        def _():
            wait(kept_x(True))

        backward_input(k, l, grad)

        @pl.when(n == 0)
        def _():
            start(kept_x(True))

        now(SECOND, 1, False)
        now(FIRST, 0, True)
        now(THIRD, 1, True)
        return carry

    lax.fori_loop(0, LAYERS, backward, 0)
    if alone:
        start(stores)
        small_stage(k, k.small_out, grad)
        wait(stores)
        return
    small_stage(k, sums.whole(), grad)
    sums.start()
    reduce.last(0, 2, k.shard, k.squares_sum)
    reduce.second(0, 0)
    sums.step(0)
    reduce.third(0, 0, k.shard)
    sums.step(1)
    reduce.last(0, 1, k.shard, k.squares_sum)
    sums.step(2)
    reduce.last(0, 0, k.shard, k.squares_sum)
    squares = k.squares_sum[...]
    norm.start(sum(squares[:, n * 128 : (n + 1) * 128] for n in range(D // 128)))
    sums.back()
    norm.step()
    sums.last()
    k.small_out[...] = sums.whole()[...]
    k.squares[...] = norm.last()


def train_pass(inputs, weights, alone):
    whole = pl.BlockSpec(memory_space=pltpu.VMEM)
    scalars = pl.BlockSpec(memory_space=pltpu.SMEM)
    anywhere = pl.BlockSpec(memory_space=pl.ANY)
    dma = pltpu.SemaphoreType.DMA
    count = PARTS * LAYERS
    names = ["states", "actions", "returns", "starts", "repeats", "valid"]
    names += ["log_temp", "small", "head_bias"]
    out_shape = {"small_out": ((SMALL, D), WIDE)}
    for name in KEEP:
        shape, dtype = WORK_SHAPES[name]
        out_shape["keep_" + name] = ((LAYERS - 1,) + shape, dtype)
    out_shape["keep_x"] = ((ROWS, D), WIDE)
    scratch = {name: pltpu.VMEM(*shape) for name, shape in WORK_SHAPES.items()}
    scratch["keep_sem"] = dma((len(KEEP) + 1,))
    if alone:
        names += ["all_a", "all_f"]
        out_shape["grad_a"] = ((LAYERS, 4, 8, ATTN, D), LOWER)
        out_shape["grad_f"] = ((LAYERS, 4, 8, FFN, D), LOWER)
        scratch["load_sem"] = dma((count,))
    else:
        names += ["qkv_w", "out_w", "up_w", "down_w"]
        out_shape["shard"] = ((LAYERS, PACK, D), WIDE)
        out_shape["squares"] = ((8, 128), WIDE)
        for part in range(PARTS):
            for n, shape in enumerate(LANDING):
                scratch["land_%d_%d" % (part, n)] = pltpu.VMEM(shape, LOWER)
        scratch["stage_sem"] = dma((LAYERS, 9))
        scratch["squares_sum"] = pltpu.VMEM((8, D), WIDE)
        for name, copies in (("gather", Gather.COPIES), ("reduce", Reduce.COPIES)):
            scratch[name + "_send"] = dma((count, copies))
            scratch[name + "_recv"] = dma((count, copies))
        scratch["credit"] = pltpu.SemaphoreType.REGULAR((PARTS, 8))
        scratch["norm_plane"] = pltpu.VMEM((8, 8, 128), WIDE)
        scratch["norm_column"] = pltpu.VMEM((NZ, 8, 128), WIDE)
        for name, copies in (("sum", Total.COPIES), ("norm", Norm.COPIES)):
            scratch[name + "_send"] = dma((copies,))
            scratch[name + "_recv"] = dma((copies,))
    spaces = dict.fromkeys(("starts", "repeats", "head_bias", "log_temp"), scalars)
    for name in ("all_a", "all_f", "grad_a", "grad_f", "qkv_w", "out_w", "up_w", "down_w"):
        spaces[name] = anywhere
    for name in KEEP + ("x",):
        spaces["keep_" + name] = anywhere
    every = names + list(out_shape) + list(scratch)

    def kernel(*given):
        refs = dict(zip(every, given))
        refs["landing"] = [
            [refs.get("land_%d_%d" % (part, n)) for n in range(len(LANDING))] for part in range(PARTS)
        ]
        train_kernel(refs, alone)

    results = pl.pallas_call(
        kernel,
        name="train_pass",
        out_shape=tuple(jax.ShapeDtypeStruct(*shape) for shape in out_shape.values()),
        in_specs=[spaces.get(name, whole) for name in names],
        out_specs=tuple(spaces.get(name, whole) for name in out_shape),
        scratch_shapes=list(scratch.values()),
        compiler_params=pltpu.CompilerParams(
            vmem_limit_bytes=VMEM_BYTES,
            collective_id=None if alone else 0,
            has_side_effects=not alone,
        ),
        cost_estimate=pl.CostEstimate(
            flops=6 * 10**10, bytes_accessed=4 * 10**7, transcendentals=10**7
        ),
    )(*inputs, *weights)
    return dict(zip(out_shape, results))


def adam_parts(weight, grad, first, second, rate):
    first = BETA_ONE * first + (1.0 - BETA_ONE) * grad
    second = BETA_TWO * second + (1.0 - BETA_TWO) * grad * grad
    fix_one = 1.0 - BETA_ONE**STEP
    fix_two = 1.0 - BETA_TWO**STEP
    fresh = weight - rate * (
        first * (1.0 / fix_one) / (jnp.sqrt(second * (1.0 / fix_two)) + ADAM_EPS) + DECAY * weight
    )
    return fresh, first, second


def adam_kernel(*refs):
    shard, small_grad, squares, groups, log_temp = refs[:5]
    small, small_first, small_second, bias, bias_first, bias_second = refs[5:11]
    mats, firsts, seconds = refs[11:15], refs[15:19], refs[19:23]
    totals, norm, next_temp, s_next, s_first, s_second, b_next, b_first, b_second = refs[23:32]
    m_next, m_copy, m_first, m_second = refs[32:36], refs[36:40], refs[40:44], refs[44:48]
    extra = small_grad[NROWS : NROWS + 3, 0:128]
    lane = iota((1, 128), 1)
    bias_mean = jnp.where(lane < A, extra[1:2], 0.0)
    bias_spread = jnp.where(lane < A, extra[2:3], 0.0)

    def all_sum(v):
        return jnp.sum(jnp.sum(v, 0, keepdims=True), 1, keepdims=True)

    grads = small_grad[0:NROWS, :]
    square = (
        all_sum(squares[0:1, :])
        + all_sum(grads * grads)
        + all_sum(bias_mean * bias_mean)
        + all_sum(bias_spread * bias_spread)
    )
    length = jnp.sqrt(square)
    clip = jnp.minimum(1.0, CLIP / (length + 1e-06))

    def rate_of(l, kind):
        group = jnp.full((1, 1), groups[l, kind], jnp.int32).astype(WIDE)
        return LEARN * jnp.exp2(-group)

    def update(l, kind, rows, cols, grad):
        at = (l, rows, cols)
        fresh, first, second = adam_parts(
            mats[kind][at], clip * grad, firsts[kind][at], seconds[kind][at], rate_of(l, kind)
        )
        m_next[kind][at] = fresh
        m_copy[kind][at] = fresh.astype(LOWER)
        m_first[kind][at] = first
        m_second[kind][at] = second

    every = slice(0, 16)
    for l in range(LAYERS):
        for j in range(3):
            update(l, 0, every, slice(j * D, (j + 1) * D), shard[l, 16 * j : 16 * j + 16, :])
        update(l, 1, every, slice(0, D), shard[l, 48:64, :])
        for j in range(4):
            rows = slice(64 + 16 * j, 80 + 16 * j)
            update(l, 2, every, slice(j * D, (j + 1) * D), shard[l, rows, :])
        update(l, 3, slice(0, 64), slice(0, D), shard[l, 128:192, :])

    s_next[...], s_first[...], s_second[...] = adam_parts(
        small[...], clip * grads, small_first[...], small_second[...], LEARN
    )

    def scalar(v, n):
        return jnp.sum(jnp.where(lane == n, v, 0.0))

    def row(ref):
        v = jnp.zeros((1, 128), WIDE)
        for n in range(2 * A):
            v = jnp.where(lane == n, ref[n], v)
        return v

    grad = bias_mean + pltpu.roll(bias_spread, A, 1)
    results = adam_parts(row(bias), clip * grad, row(bias_first), row(bias_second), LEARN)
    for ref, result in zip((b_next, b_first, b_second), results):
        for n in range(2 * A):
            ref[n] = scalar(result, n)
    sums = extra[0:1]
    for n in range(3):
        totals[n] = scalar(sums, n)
    norm[0] = jnp.sum(length)
    logs = jnp.full((1, 1), log_temp[0], WIDE)
    ratio = jnp.full((1, 1), scalar(sums, 1), WIDE) / jnp.full((1, 1), scalar(sums, 2), WIDE)
    next_temp[0] = jnp.sum(logs - TEMP_RATE * jnp.exp(logs) * (ratio + A))


def adam_all(shard, small_grad, squares, groups, log_temp, smalls, biases, mats, firsts, seconds):
    scalars = pl.BlockSpec(memory_space=pltpu.SMEM)

    whole = pl.BlockSpec(memory_space=pltpu.VMEM)

    def like(array, dtype=WIDE):
        return jax.ShapeDtypeStruct(array.shape, dtype)

    stacks = list(mats) + list(firsts) + list(seconds)
    small, bias = smalls[0], biases[0]
    return pl.pallas_call(
        adam_kernel,
        name="adam",
        out_shape=(
            (jax.ShapeDtypeStruct((3,), WIDE),)
            + (jax.ShapeDtypeStruct((1,), WIDE),) * 2
            + (like(small),) * 3
            + (like(bias),) * 3
            + tuple(like(m) for m in mats)
            + tuple(like(m, LOWER) for m in mats)
            + tuple(like(m) for m in mats) * 2
        ),
        in_specs=[whole] * 3 + [scalars] * 2 + [whole] * 3 + [scalars] * 3 + [whole] * 12,
        out_specs=(scalars,) * 3 + (whole,) * 3 + (scalars,) * 3 + (whole,) * 16,
        compiler_params=pltpu.CompilerParams(vmem_limit_bytes=VMEM_BYTES),
        cost_estimate=pl.CostEstimate(flops=10**7, bytes_accessed=8 * 10**6, transcendentals=10**6),
    )(shard, small_grad, squares, groups, log_temp, *smalls, *biases, *stacks)


def gather_packed(mats, axes, count):
    group = count // BLOCKS
    pieces = []
    for mat in mats:
        rows, wide = mat.shape[1], mat.shape[2] // D
        piece = mat.astype(LOWER).reshape(LAYERS, rows, wide, D)
        piece = lax.all_gather(piece, axes, axis=1, tiled=True)
        piece = piece.reshape(LAYERS, NZ, NY, NX, NC, group * rows, wide, D)
        piece = piece.transpose(0, 4, 3, 2, 1, 6, 5, 7)
        pieces.append(piece.reshape(LAYERS, 4, 8, wide * group * rows, D))
    return jnp.concatenate(pieces[:2], 3), jnp.concatenate(pieces[2:], 3)


def scatter_packed(grads, mats, axes):
    results, first = [], 0
    for n, mat in enumerate(mats):
        rows, wide = mat.shape[1], mat.shape[2] // D
        total = lax.psum(1, axes) * rows
        deep = total // BLOCKS
        first = 0 if n % 2 == 0 else first
        piece = grads[n // 2][:, :, :, first : first + wide * deep].astype(WIDE)
        first += wide * deep
        piece = piece.reshape(LAYERS, NC, NX, NY, NZ, wide, deep, D)
        piece = piece.transpose(0, 4, 3, 2, 1, 6, 5, 7).reshape(LAYERS, total, wide * D)
        results.append(lax.psum_scatter(piece, axes, scatter_dimension=1, tiled=True))
    return results


def local(
    buf_states,
    buf_actions,
    buf_returns,
    window_starts,
    window_repeats,
    valid_steps,
    matrix_groups,
    log_temp,
    small_rows,
    head_bias,
    qkv_weight,
    out_weight,
    up_weight,
    down_weight,
    small_first,
    bias_first,
    qkv_first,
    out_first,
    up_first,
    down_first,
    small_second,
    bias_second,
    qkv_second,
    out_second,
    up_second,
    down_second,
):
    axes = ("dp", "fsdp")
    mats = (qkv_weight, out_weight, up_weight, down_weight)
    firsts = (qkv_first, out_first, up_first, down_first)
    seconds = (qkv_second, out_second, up_second, down_second)
    pass_inputs = (
        buf_states.T,
        buf_actions.T,
        buf_returns[None],
        window_starts,
        window_repeats,
        valid_steps,
        log_temp,
        small_rows,
        head_bias,
    )
    if FF // down_weight.shape[1] == BLOCKS and lax.psum(1, "fsdp") == NX * NC:
        made = train_pass(pass_inputs, mats, False)
        return adam_all(
            made["shard"],
            made["small_out"],
            made["squares"],
            matrix_groups,
            log_temp,
            (small_rows, small_first, small_second),
            (head_bias, bias_first, bias_second),
            mats,
            firsts,
            seconds,
        )
    packed = gather_packed(mats, axes, FF // down_weight.shape[1])
    made = train_pass(pass_inputs, packed, True)
    big = scatter_packed((made["grad_a"], made["grad_f"]), mats, axes)
    small = made["small_out"]
    small = lax.psum(small, axes)
    small_grad, totals = small[:NROWS], small[NROWS, :3]
    bias_grad = jnp.concatenate([small[NROWS + 1, :A], small[NROWS + 2, :A]])
    square = sum((jnp.sum(piece * piece) for piece in big))
    square = (
        lax.psum(square, axes) + jnp.sum(small_grad * small_grad) + jnp.sum(bias_grad * bias_grad)
    )
    grad_norm = jnp.sqrt(square)
    clip = jnp.minimum(1.0, CLIP / (grad_norm + 1e-06))
    rates = LEARN * jnp.exp2(-matrix_groups.astype(WIDE))
    results = [
        adam_parts(
            mats[kind], clip * big[kind], firsts[kind], seconds[kind], rates[:, kind][:, None, None]
        )
        for kind in range(4)
    ]
    small_new = adam_parts(small_rows, clip * small_grad, small_first, small_second, LEARN)
    bias_new = adam_parts(head_bias, clip * bias_grad, bias_first, bias_second, LEARN)
    next_temp = log_temp - TEMP_RATE * jnp.exp(log_temp) * (totals[1] / totals[2] + A)
    return (
        (totals, grad_norm[None], next_temp)
        + small_new
        + bias_new
        + tuple(r[0] for r in results)
        + tuple(r[0].astype(LOWER) for r in results)
        + tuple(r[1] for r in results)
        + tuple(r[2] for r in results)
    )


def solution(mesh):
    rows = P(("dp", "fsdp"), None)
    vector = P(("dp", "fsdp"))
    stack = P(None, ("dp", "fsdp"), None)
    same = P()
    in_specs = (
        (rows, rows, vector, vector, vector, rows)
        + (same,) * 4
        + (stack,) * 4
        + (same,) * 2
        + (stack,) * 4
        + (same,) * 2
        + (stack,) * 4
    )
    out_specs = (same,) * 9 + (stack,) * 16
    return jax.shard_map(local, mesh=mesh, in_specs=in_specs, out_specs=out_specs, check_vma=False)
```

profile of v0, /device:TPU:0, one launch (start us, length us, event | category | flops | bytes accessed | tf_op | source)
XLA Modules:
  0.0 253.9 jit_solution(12752675457739740796)
XLA Ops:
  1.3 246.4 %train_pass.1 = (f32[96,512]{1,0:T(8,128)}, bf16[2,1024,1536]{2,1,0:T(8,128)(2,1)}, bf16[2,512,1024]{2,1,0:T(8,128)(2,1)}, bf16[2,512,1024]{2,1,0:T(8,128)(2,1)}...) custom-call(f32[11,64]{1,0:T(8,128)} %bitcast.3, ...), custom_call_target="tpu_custom_call" | custom-call | flops 60000002048 | bytes 40000000 | tf_op jit(solution)/shard_map/train_pass/pallas_call | solution.py:1317
  247.7 6.1 %adam.1 = (f32[3]{0:T(128)}, f32[1]{0:T(128)}, f32[1]{0:T(128)}, f32[85,512]{1,0:T(8,128)}, f32[85,512]{1,0:T(8,128)}, /*index=5*/f32[85,512]{1,0:T(8,128)}, f32...) custom-call(f32[3,192,512]{2,1,0:T(8,128)} %get-tuple-element.28.ref, ...), custom_call_target="tpu_custom_call" | custom-call | flops 10000000 | bytes 8000000 | tf_op jit(solution)/shard_map/adam/pallas_call | solution.py:1432
where the time goes:
time: 254 us
  Pallas kernels  252 us (99%)
    pallas_call x1, Pallas kernels, train_pass(): pl.pallas_call(kernel, name='train_pass', out_shape=tuple((jax.ShapeDtype...  246 us
    pallas_call x1, Pallas kernels, adam_all(): pl.pallas_call(adam_kernel, name='adam', out_shape=(jax.ShapeDtypeStruct(...  6.06 us

commit v1 on v0

--- a/solution.py
+++ b/solution.py
@@ -930,29 +930,28 @@
 BEGIN, SETUP, START, QKV_HALF, QKV, WINDOWS_HALF, WINDOWS, UP_HALF, UP, DOWN = range(10)
 FIRST, SECOND, THIRD, FOURTH, FIFTH, LAST, SEND = range(7)
 GATHER_PLAN = {
-    (-1, BEGIN): [(FIRST, 0, 0), (FIRST, 0, 1), (FIRST, 0, 2)],
-    (-1, SETUP): [(FIRST, 1, 0), (FIRST, 1, 1), (SECOND, 0, 0)],
-    (0, START): [(FIRST, 1, 2), (SECOND, 0, 1), (THIRD, 0, 0), (FOURTH, 0, 0), (SECOND, 0, 2), (THIRD, 0, 1), (FIFTH, 0, 0), (LAST, 0, 0)],
-    (0, QKV_HALF): [(SECOND, 1, 0), (FOURTH, 0, 1)],
-    (0, QKV): [(FIRST, 2, 0), (THIRD, 0, 2), (FIFTH, 0, 1)],
-    (0, WINDOWS_HALF): [(SECOND, 1, 1), (LAST, 0, 1)],
-    (0, WINDOWS): [(FIRST, 2, 1), (FOURTH, 0, 2)],
-    (0, UP_HALF): [(THIRD, 1, 0), (FIFTH, 0, 2), (SECOND, 1, 2)],
-    (0, UP): [(FIRST, 2, 2), (LAST, 0, 2), (FOURTH, 1, 0), (SECOND, 2, 0)],
-    (0, DOWN): [(THIRD, 1, 1), (FIFTH, 1, 0)],
-    (1, START): [(LAST, 1, 0), (FOURTH, 1, 1)],
-    (1, QKV_HALF): [(SECOND, 2, 1)],
-    (1, QKV): [(THIRD, 1, 2), (FIFTH, 1, 1)],
-    (1, WINDOWS_HALF): [(LAST, 1, 1)],
-    (1, WINDOWS): [(SECOND, 2, 2), (FOURTH, 1, 2)],
-    (1, UP_HALF): [(THIRD, 2, 0), (FIFTH, 1, 2), (LAST, 1, 2)],
-    (1, UP): [(FOURTH, 2, 0)],
-    (1, DOWN): [(THIRD, 2, 1), (FIFTH, 2, 0)],
-    (2, START): [(LAST, 2, 0), (FOURTH, 2, 1)],
-    (2, QKV): [(THIRD, 2, 2), (FIFTH, 2, 1)],
-    (2, WINDOWS_HALF): [(LAST, 2, 1)],
-    (2, WINDOWS): [(FOURTH, 2, 2)],
-    (2, UP): [(FIFTH, 2, 2), (LAST, 2, 2)],
+    (-1, BEGIN): [(FIRST, 0, 0), (FIRST, 0, 1)],
+    (-1, SETUP): [(SECOND, 0, 0), (FIRST, 0, 2)],
+    (0, START): [(THIRD, 0, 0), (SECOND, 0, 1), (FOURTH, 0, 0), (FIRST, 1, 0), (FIFTH, 0, 0), (LAST, 0, 0)],
+    (0, QKV_HALF): [(SECOND, 0, 2), (THIRD, 0, 1), (FIRST, 1, 1)],
+    (0, QKV): [(FOURTH, 0, 1), (SECOND, 1, 0), (FIRST, 1, 2)],
+    (0, WINDOWS_HALF): [(FIFTH, 0, 1), (THIRD, 0, 2), (LAST, 0, 1), (SECOND, 1, 1), (FIRST, 2, 0)],
+    (0, WINDOWS): [(FOURTH, 0, 2), (THIRD, 1, 0)],
+    (0, UP_HALF): [(FIFTH, 0, 2), (SECOND, 1, 2), (FIRST, 2, 1), (FOURTH, 1, 0)],
+    (0, UP): [(LAST, 0, 2), (THIRD, 1, 1), (FIFTH, 1, 0), (SECOND, 2, 0)],
+    (0, DOWN): [(FIRST, 2, 2), (FOURTH, 1, 1)],
+    (1, START): [(LAST, 1, 0)],
+    (1, QKV_HALF): [(SECOND, 2, 1), (THIRD, 1, 2)],
+    (1, QKV): [(FIFTH, 1, 1)],
+    (1, WINDOWS_HALF): [(LAST, 1, 1), (SECOND, 2, 2), (FOURTH, 1, 2), (THIRD, 2, 0)],
+    (1, WINDOWS): [(FIFTH, 1, 2)],
+    (1, UP_HALF): [(LAST, 1, 2), (FOURTH, 2, 0)],
+    (1, UP): [(THIRD, 2, 1), (FIFTH, 2, 0)],
+    (1, DOWN): [(LAST, 2, 0), (FOURTH, 2, 1)],
+    (2, QKV_HALF): [(THIRD, 2, 2), (FIFTH, 2, 1)],
+    (2, QKV): [(FOURTH, 2, 2)],
+    (2, WINDOWS_HALF): [(LAST, 2, 1), (FIFTH, 2, 2)],
+    (2, WINDOWS): [(LAST, 2, 2)],
 }
 
 
@@ -1347,9 +1346,19 @@
 def adam_kernel(*refs):
     shard, small_grad, squares, groups, log_temp = refs[:5]
     small, small_first, small_second, bias, bias_first, bias_second = refs[5:11]
-    mats, firsts, seconds = refs[11:15], refs[15:19], refs[19:23]
+    far_in, far_out = refs[11:23], refs[32:48]
+    near_in, near_out, load, store = refs[48:60], refs[60:76], refs[76], refs[77]
+    loads = [pltpu.make_async_copy(a, b, load.at[n]) for n, (a, b) in enumerate(zip(far_in, near_in))]
+    stores = [
+        pltpu.make_async_copy(a, b, store.at[n]) for n, (a, b) in enumerate(zip(near_out, far_out))
+    ]
+    kinds = (3, 2, 0, 1)
+    for kind in kinds:
+        for n in range(3):
+            loads[4 * n + kind].start()
+    mats, firsts, seconds = near_in[0:4], near_in[4:8], near_in[8:12]
     totals, norm, next_temp, s_next, s_first, s_second, b_next, b_first, b_second = refs[23:32]
-    m_next, m_copy, m_first, m_second = refs[32:36], refs[36:40], refs[40:44], refs[44:48]
+    m_next, m_copy, m_first, m_second = [near_out[4 * n : 4 * n + 4] for n in range(4)]
     extra = small_grad[NROWS : NROWS + 3, 0:128]
     lane = iota((1, 128), 1)
     bias_mean = jnp.where(lane < A, extra[1:2], 0.0)
@@ -1382,15 +1391,20 @@
         m_first[kind][at] = first
         m_second[kind][at] = second
 
-    every = slice(0, 16)
-    for l in range(LAYERS):
-        for j in range(3):
-            update(l, 0, every, slice(j * D, (j + 1) * D), shard[l, 16 * j : 16 * j + 16, :])
-        update(l, 1, every, slice(0, D), shard[l, 48:64, :])
-        for j in range(4):
-            rows = slice(64 + 16 * j, 80 + 16 * j)
-            update(l, 2, every, slice(j * D, (j + 1) * D), shard[l, rows, :])
-        update(l, 3, slice(0, 64), slice(0, D), shard[l, 128:192, :])
+    every, wide = slice(0, 16), (3, 1, 4)
+    for kind in kinds:
+        for n in range(3):
+            loads[4 * n + kind].wait()
+        for l in range(LAYERS):
+            if kind == 3:
+                update(l, 3, slice(0, 64), slice(0, D), shard[l, 128:192, :])
+                continue
+            for j in range(wide[kind]):
+                row = (0, 48, 64)[kind] + 16 * j
+                cols = slice(j * D, (j + 1) * D)
+                update(l, kind, every, cols, shard[l, row : row + 16, :])
+        for n in range(4):
+            stores[4 * n + kind].start()
 
     s_next[...], s_first[...], s_second[...] = adam_parts(
         small[...], clip * grads, small_first[...], small_second[...], LEARN
@@ -1417,12 +1431,15 @@
     logs = jnp.full((1, 1), log_temp[0], WIDE)
     ratio = jnp.full((1, 1), scalar(sums, 1), WIDE) / jnp.full((1, 1), scalar(sums, 2), WIDE)
     next_temp[0] = jnp.sum(logs - TEMP_RATE * jnp.exp(logs) * (ratio + A))
+    for copy in stores:
+        copy.wait()
 
 
 def adam_all(shard, small_grad, squares, groups, log_temp, smalls, biases, mats, firsts, seconds):
     scalars = pl.BlockSpec(memory_space=pltpu.SMEM)
 
     whole = pl.BlockSpec(memory_space=pltpu.VMEM)
+    anywhere = pl.BlockSpec(memory_space=pl.ANY)
 
     def like(array, dtype=WIDE):
         return jax.ShapeDtypeStruct(array.shape, dtype)
@@ -1441,8 +1458,11 @@
             + tuple(like(m, LOWER) for m in mats)
             + tuple(like(m) for m in mats) * 2
         ),
-        in_specs=[whole] * 3 + [scalars] * 2 + [whole] * 3 + [scalars] * 3 + [whole] * 12,
-        out_specs=(scalars,) * 3 + (whole,) * 3 + (scalars,) * 3 + (whole,) * 16,
+        in_specs=[whole] * 3 + [scalars] * 2 + [whole] * 3 + [scalars] * 3 + [anywhere] * 12,
+        out_specs=(scalars,) * 3 + (whole,) * 3 + (scalars,) * 3 + (anywhere,) * 16,
+        scratch_shapes=[pltpu.VMEM(a.shape, WIDE) for a in stacks]
+        + [pltpu.VMEM(m.shape, dtype) for dtype in (WIDE, LOWER, WIDE, WIDE) for m in mats]
+        + [pltpu.SemaphoreType.DMA((12,)), pltpu.SemaphoreType.DMA((16,))],
         compiler_params=pltpu.CompilerParams(vmem_limit_bytes=VMEM_BYTES),
         cost_estimate=pl.CostEstimate(flops=10**7, bytes_accessed=8 * 10**6, transcendentals=10**6),
     )(shard, small_grad, squares, groups, log_temp, *smalls, *biases, *stacks)

time: 254 us -> 252 us (level)
    pallas_call x1, Pallas kernels: 246 us -> 243 us  [train_pass(): pl.pallas_call(kernel, name='train_pass', out_shape=tuple((jax.ShapeDtype...]
where the time goes in v1:
time: 252 us; the launch traced here: 251 us
  Pallas kernels  250 us (99%)
    pallas_call x1, Pallas kernels, train_pass(): pl.pallas_call(kernel, name='train_pass', out_shape=tuple((jax.ShapeDtype...  243 us
    pallas_call x1, Pallas kernels, adam_all(): pl.pallas_call(adam_kernel, name='adam', out_shape=(jax.ShapeDtypeStruct(...  6.41 us

profile of v1, /device:TPU:0, one launch (start us, length us, event | category | flops | bytes accessed | tf_op | source)
XLA Modules:
  0.0 251.4 jit_solution(12603202976800897261)
XLA Ops:
  1.3 243.5 %train_pass.1 = (f32[96,512]{1,0:T(8,128)}, bf16[2,1024,1536]{2,1,0:T(8,128)(2,1)}, bf16[2,512,1024]{2,1,0:T(8,128)(2,1)}, bf16[2,512,1024]{2,1,0:T(8,128)(2,1)}...) custom-call(f32[11,64]{1,0:T(8,128)} %bitcast.3, ...), custom_call_target="tpu_custom_call" | custom-call | flops 60000002048 | bytes 40000000 | tf_op jit(solution)/shard_map/train_pass/pallas_call | solution.py:1316
  244.8 6.4 %adam.1 = (f32[3]{0:T(128)}, f32[1]{0:T(128)}, f32[1]{0:T(128)}, f32[85,512]{1,0:T(8,128)}, f32[85,512]{1,0:T(8,128)}, /*index=5*/f32[85,512]{1,0:T(8,128)}, f32...) custom-call(f32[3,192,512]{2,1,0:T(8,128)} %get-tuple-element.28.ref, ...), custom_call_target="tpu_custom_call" | custom-call | flops 10000000 | bytes 8000000 | tf_op jit(solution)/shard_map/adam/pallas_call | solution.py:1449

commit v2 on v0

--- a/solution.py
+++ b/solution.py
@@ -149,6 +149,10 @@
     k.headw[1, 0:A, :] = k.small[HEADW + A : HEADW + 2 * A, :].astype(LOWER)
     for l in range(LAYERS):
         k.lrows[l, 0:PER, :] = k.small[BASE + l * PER : BASE + (l + 1) * PER, :]
+    low_half = iota((SLOT, 128), 1) < HD
+    for n, factor in enumerate((HD**-0.5, 1.0)):
+        k.pairs[2 * n] = jnp.where(low_half, factor, 0.0).astype(LOWER)
+        k.pairs[2 * n + 1] = jnp.where(low_half, 0.0, factor).astype(LOWER)
     k.sgl[...] = jnp.zeros_like(k.sgl)
     k.sgh[...] = jnp.zeros_like(k.sgh)
     k.sgw[...] = jnp.zeros_like(k.sgw)
@@ -201,9 +205,8 @@
     lax.fori_loop(0, CHUNKS, chunk, 0)
 
 
-def stack_pair(v, first):
-    zero = jnp.zeros_like(v)
-    return jnp.concatenate([jnp.where(first, v, zero), jnp.where(first, zero, v)], 0)
+def stack_pair(v, masks):
+    return jnp.concatenate([v * masks[0], v * masks[1]], 0)
 
 
 def join_pair(v, first):
@@ -265,10 +268,10 @@
 
 def forward_windows(k, l, between):
     first = iota((SLOT, 128), 1) < HD
-    scale = jnp.asarray(HD**-0.5, LOWER)
+    scaled = (k.pairs[0], k.pairs[1])
 
     def pair(both, chains):
-        query = [stack_pair(qkv_part(k, 0, rows, at) * scale, first) for _, rows, at in chains]
+        query = [stack_pair(qkv_part(k, 0, rows, at), scaled) for _, rows, at in chains]
         scores = [
             dot_nt(qkv_part(k, 1, rows, at), q) + k.bias[rows, :]
             for q, (_, rows, at) in zip(query, chains)
@@ -480,11 +483,11 @@
 def backward_windows(k, l, between):
     first = iota((SLOT, 128), 1) < HD
     scale = HD**-0.5
-    low = jnp.asarray(scale, LOWER)
+    scaled, plain = (k.pairs[0], k.pairs[1]), (k.pairs[2], k.pairs[3])
 
     def pair(both, chains):
-        query = [stack_pair(qkv_part(k, 0, rows, at) * low, first) for _, rows, at in chains]
-        d_mixed = [stack_pair(k.dout[rows, at], first) for _, rows, at in chains]
+        query = [stack_pair(qkv_part(k, 0, rows, at), scaled) for _, rows, at in chains]
+        d_mixed = [stack_pair(k.dout[rows, at], plain) for _, rows, at in chains]
         shift = [
             k.bias[rows, :] - k.logs[l, w, at.start // 128 : at.start // 128 + 1, :]
             for w, rows, at in chains
@@ -556,6 +559,7 @@
     feats=((ROWS, 128), WIDE),
     heads=((STATES, 128), WIDE),
     bias=((ROWS, 128), WIDE),
+    pairs=((4, SLOT, 128), LOWER),
     headw=((2, 128, D), LOWER),
     lrows=((LAYERS, 16, D), WIDE),
     sgl=((LAYERS, 16, D), WIDE),
@@ -930,29 +934,28 @@
 BEGIN, SETUP, START, QKV_HALF, QKV, WINDOWS_HALF, WINDOWS, UP_HALF, UP, DOWN = range(10)
 FIRST, SECOND, THIRD, FOURTH, FIFTH, LAST, SEND = range(7)
 GATHER_PLAN = {
-    (-1, BEGIN): [(FIRST, 0, 0), (FIRST, 0, 1), (FIRST, 0, 2)],
-    (-1, SETUP): [(FIRST, 1, 0), (FIRST, 1, 1), (SECOND, 0, 0)],
-    (0, START): [(FIRST, 1, 2), (SECOND, 0, 1), (THIRD, 0, 0), (FOURTH, 0, 0), (SECOND, 0, 2), (THIRD, 0, 1), (FIFTH, 0, 0), (LAST, 0, 0)],
-    (0, QKV_HALF): [(SECOND, 1, 0), (FOURTH, 0, 1)],
-    (0, QKV): [(FIRST, 2, 0), (THIRD, 0, 2), (FIFTH, 0, 1)],
-    (0, WINDOWS_HALF): [(SECOND, 1, 1), (LAST, 0, 1)],
-    (0, WINDOWS): [(FIRST, 2, 1), (FOURTH, 0, 2)],
-    (0, UP_HALF): [(THIRD, 1, 0), (FIFTH, 0, 2), (SECOND, 1, 2)],
-    (0, UP): [(FIRST, 2, 2), (LAST, 0, 2), (FOURTH, 1, 0), (SECOND, 2, 0)],
-    (0, DOWN): [(THIRD, 1, 1), (FIFTH, 1, 0)],
-    (1, START): [(LAST, 1, 0), (FOURTH, 1, 1)],
-    (1, QKV_HALF): [(SECOND, 2, 1)],
-    (1, QKV): [(THIRD, 1, 2), (FIFTH, 1, 1)],
-    (1, WINDOWS_HALF): [(LAST, 1, 1)],
-    (1, WINDOWS): [(SECOND, 2, 2), (FOURTH, 1, 2)],
-    (1, UP_HALF): [(THIRD, 2, 0), (FIFTH, 1, 2), (LAST, 1, 2)],
-    (1, UP): [(FOURTH, 2, 0)],
-    (1, DOWN): [(THIRD, 2, 1), (FIFTH, 2, 0)],
-    (2, START): [(LAST, 2, 0), (FOURTH, 2, 1)],
-    (2, QKV): [(THIRD, 2, 2), (FIFTH, 2, 1)],
-    (2, WINDOWS_HALF): [(LAST, 2, 1)],
-    (2, WINDOWS): [(FOURTH, 2, 2)],
-    (2, UP): [(FIFTH, 2, 2), (LAST, 2, 2)],
+    (-1, BEGIN): [(FIRST, 0, 0), (FIRST, 0, 1)],
+    (-1, SETUP): [(SECOND, 0, 0), (FIRST, 0, 2)],
+    (0, START): [(THIRD, 0, 0), (SECOND, 0, 1), (FOURTH, 0, 0), (FIRST, 1, 0), (FIFTH, 0, 0), (LAST, 0, 0)],
+    (0, QKV_HALF): [(SECOND, 0, 2), (THIRD, 0, 1), (FIRST, 1, 1)],
+    (0, QKV): [(FOURTH, 0, 1), (SECOND, 1, 0), (FIRST, 1, 2)],
+    (0, WINDOWS_HALF): [(FIFTH, 0, 1), (THIRD, 0, 2), (LAST, 0, 1), (SECOND, 1, 1), (FIRST, 2, 0)],
+    (0, WINDOWS): [(FOURTH, 0, 2), (THIRD, 1, 0)],
+    (0, UP_HALF): [(FIFTH, 0, 2), (SECOND, 1, 2), (FIRST, 2, 1), (FOURTH, 1, 0)],
+    (0, UP): [(LAST, 0, 2), (THIRD, 1, 1), (FIFTH, 1, 0), (SECOND, 2, 0)],
+    (0, DOWN): [(FIRST, 2, 2), (FOURTH, 1, 1)],
+    (1, START): [(LAST, 1, 0)],
+    (1, QKV_HALF): [(SECOND, 2, 1), (THIRD, 1, 2)],
+    (1, QKV): [(FIFTH, 1, 1)],
+    (1, WINDOWS_HALF): [(LAST, 1, 1), (SECOND, 2, 2), (FOURTH, 1, 2), (THIRD, 2, 0)],
+    (1, WINDOWS): [(FIFTH, 1, 2)],
+    (1, UP_HALF): [(LAST, 1, 2), (FOURTH, 2, 0)],
+    (1, UP): [(THIRD, 2, 1), (FIFTH, 2, 0)],
+    (1, DOWN): [(LAST, 2, 0), (FOURTH, 2, 1)],
+    (2, QKV_HALF): [(THIRD, 2, 2), (FIFTH, 2, 1)],
+    (2, QKV): [(FOURTH, 2, 2)],
+    (2, WINDOWS_HALF): [(LAST, 2, 1), (FIFTH, 2, 2)],
+    (2, WINDOWS): [(LAST, 2, 2)],
 }
 
 

time: 254 us -> 251 us (0.988)
    pallas_call x1, Pallas kernels: 246 us -> 243 us  [train_pass(): pl.pallas_call(kernel, name='train_pass', out_shape=tuple((jax.ShapeDtype...]
where the time goes in v2:
time: 251 us
  Pallas kernels  250 us (100%)
    pallas_call x1, Pallas kernels, train_pass(): pl.pallas_call(kernel, name='train_pass', out_shape=tuple((jax.ShapeDtype...  243 us
    pallas_call x1, Pallas kernels, adam_all(): pl.pallas_call(adam_kernel, name='adam', out_shape=(jax.ShapeDtypeStruct(...  6.06 us

profile of v2, /device:TPU:0, one launch (start us, length us, event | category | flops | bytes accessed | tf_op | source)
XLA Modules:
  0.0 251.0 jit_solution(1416231093505731989)
XLA Ops:
  1.3 243.5 %train_pass.1 = (f32[96,512]{1,0:T(8,128)}, bf16[2,1024,1536]{2,1,0:T(8,128)(2,1)}, bf16[2,512,1024]{2,1,0:T(8,128)(2,1)}, bf16[2,512,1024]{2,1,0:T(8,128)(2,1)}...) custom-call(f32[11,64]{1,0:T(8,128)} %bitcast.3, ...), custom_call_target="tpu_custom_call" | custom-call | flops 60000002048 | bytes 40000000 | tf_op jit(solution)/shard_map/train_pass/pallas_call | solution.py:1320
  244.8 6.1 %adam.1 = (f32[3]{0:T(128)}, f32[1]{0:T(128)}, f32[1]{0:T(128)}, f32[85,512]{1,0:T(8,128)}, f32[85,512]{1,0:T(8,128)}, /*index=5*/f32[85,512]{1,0:T(8,128)}, f32...) custom-call(f32[3,192,512]{2,1,0:T(8,128)} %get-tuple-element.28.ref, ...), custom_call_target="tpu_custom_call" | custom-call | flops 10000000 | bytes 8000000 | tf_op jit(solution)/shard_map/adam/pallas_call | solution.py:1435
